TPU v7x, 256 devices: a whole 4x4x8 slice. The times are simulated.
256 devices in a mesh: seq: 8 (over z), head: 32 (over x, y, core).
Axes of the slice: x: 4, y: 4, z: 8, core: 2. Of those that a mesh axis runs over, the one named last changes fastest.
Arguments:
- projected: bfloat16 [2, 16384, 16384], P(None, ('seq', 'head')), may hold values from -6 to 6
- state_maps: bfloat16 [2, 16384, 4096], P(None, ('seq', 'head')), may hold values from -3 to 3
- step_raw: bfloat16 [2, 16384, 256], P(None, ('seq', 'head')), may hold values from -3 to 14
- step_bias: float32 [256], P('head'), may hold values from -9 to -2
- decay_rate: float32 [256], P('head'), may hold values from 0.1 to 2
- skip_gain: float32 [256], P('head'), may hold values from 0.5 to 1.5
- conv_weight: bfloat16 [4, 16384], P(None, 'head'), may hold values from -3 to 3
- conv_bias: float32 [16384], P('head'), may hold values from -1.5 to 1.5
- map_weight: bfloat16 [4, 4096], replicated, may hold values from -3 to 3
- map_bias: float32 [4096], replicated, may hold values from -1.5 to 1.5
Outputs:
- mixed_out: bfloat16 [2, 16384, 16384], P(None, ('seq', 'head'))
All inputs are finite; a program needn't handle non-finite values.
Results may differ from a plain program's by a relative error of at most 0.0057.
Values may be sent and summed in bfloat16 or wider, within the bound.
A program may use at most 128 MiB of HBM per device.

v0:
```python
import jax
import jax.numpy as jnp
from jax import lax
from jax.sharding import PartitionSpec as P

HEAD_DIM = 64
STATE = 256
GROUPS = 8
SPAN = 256
CONV = 4


def from_behind(array, axis, by):
    count = lax.axis_size(axis)
    pairs = [(i, i + by) for i in range(count) if 0 <= i + by < count]
    return lax.ppermute(array, axis, pairs)


def causal_conv(rim_rows, inner_rows, weight, bias):
    length = inner_rows.shape[1]
    window = jnp.concatenate([rim_rows, inner_rows], axis=1)
    total = bias
    for tap_index in range(CONV):
        part = lax.slice_in_dim(window, tap_index, tap_index + length, axis=1)
        total = total + weight[tap_index].astype(jnp.float32) * part.astype(jnp.float32)
    return jax.nn.silu(total).astype(jnp.bfloat16)


def local(
    projected,
    state_maps,
    step_raw,
    step_bias,
    decay_rate,
    skip_gain,
    conv_weight,
    conv_bias,
    map_weight,
    map_bias,
):
    head_count = lax.axis_size("head")
    heads_here = step_bias.shape[0]
    seq_count = projected.shape[0]
    row_count = projected.shape[1]
    width = heads_here * HEAD_DIM
    repeats = head_count // GROUPS
    group_index = lax.axis_index("head") // repeats
    grouped = state_maps.reshape(seq_count, row_count, 2, GROUPS, STATE).transpose(0, 1, 3, 2, 4)
    spread = jnp.broadcast_to(
        grouped[:, :, :, None], (seq_count, row_count, GROUPS, repeats, 2, STATE)
    )
    sent_maps = spread.reshape(seq_count, row_count, head_count * 2 * STATE)
    local_x, local_step, local_maps = (
        lax.all_to_all(projected, "head", split_axis=2, concat_axis=1, tiled=True),
        lax.all_to_all(step_raw, "head", split_axis=2, concat_axis=1, tiled=True),
        lax.all_to_all(sent_maps, "head", split_axis=2, concat_axis=1, tiled=True),
    )
    length = local_x.shape[1]
    map_taps = lax.dynamic_slice_in_dim(
        map_weight.reshape(CONV, 2, GROUPS, STATE), group_index, 1, 2
    ).reshape(CONV, 2 * STATE)
    map_shift = lax.dynamic_slice_in_dim(
        map_bias.reshape(2, GROUPS, STATE), group_index, 1, 1
    ).reshape(2 * STATE)
    rim_x, rim_maps = from_behind(
        (local_x[:, length - CONV + 1 :], local_maps[:, length - CONV + 1 :]), "seq", 1
    )
    inner_x = causal_conv(rim_x, local_x, conv_weight, conv_bias)
    inner_maps = causal_conv(rim_maps, local_maps, map_taps, map_shift)
    delta = jax.nn.softplus(local_step.astype(jnp.float32) + step_bias)
    log_decay = -delta * decay_rate
    span_count = length // SPAN
    x_spans = inner_x.reshape(seq_count, span_count, SPAN, heads_here, HEAD_DIM)
    b_spans = inner_maps[:, :, :STATE].reshape(seq_count, span_count, SPAN, STATE)
    c_spans = inner_maps[:, :, STATE:].reshape(seq_count, span_count, SPAN, STATE)
    delta_spans = delta.reshape(seq_count, span_count, SPAN, heads_here)
    cumulative = jnp.cumsum(log_decay.reshape(seq_count, span_count, SPAN, heads_here), axis=2)
    lower = lax.broadcasted_iota(jnp.int32, (SPAN, SPAN), 0) >= lax.broadcasted_iota(
        jnp.int32, (SPAN, SPAN), 1
    )

    def span_work(index):
        x_here = lax.dynamic_index_in_dim(x_spans, index, 1, keepdims=False)
        b_here = lax.dynamic_index_in_dim(b_spans, index, 1, keepdims=False)
        c_here = lax.dynamic_index_in_dim(c_spans, index, 1, keepdims=False)
        delta_here = lax.dynamic_index_in_dim(delta_spans, index, 1, keepdims=False)
        cum_here = lax.dynamic_index_in_dim(cumulative, index, 1, keepdims=False)
        scores = jnp.einsum("stn,skn->stk", c_here, b_here, preferred_element_type=jnp.float32)
        cum_heads = cum_here.transpose(0, 2, 1)
        differ = cum_heads[:, :, :, None] - cum_heads[:, :, None, :]
        decay = jnp.where(lower, jnp.exp(jnp.minimum(differ, 0.0)), 0.0)
        weights = (scores[:, None] * decay * delta_here.transpose(0, 2, 1)[:, :, None, :]).astype(
            jnp.bfloat16
        )
        intra = jnp.einsum("shtk,skhp->sthp", weights, x_here, preferred_element_type=jnp.float32)
        scale = jnp.exp(cum_here[:, -1:] - cum_here) * delta_here
        carried = (x_here * scale[..., None]).astype(jnp.bfloat16)
        produced = jnp.einsum("skhp,skn->shpn", carried, b_here, preferred_element_type=jnp.float32)
        return (intra, produced)

    intra_all, produced_all = lax.map(span_work, jnp.arange(span_count, dtype=jnp.int32))
    totals = cumulative[:, :, -1]
    totals_first = jnp.moveaxis(totals, 1, 0)

    def advance(state_now, item):
        decay_total, produced = item
        return (jnp.exp(decay_total)[..., None, None] * state_now + produced, state_now)

    zero_state = jnp.zeros((seq_count, heads_here, HEAD_DIM, STATE), jnp.float32)
    block_end, entering_local = lax.scan(advance, zero_state, (totals_first, produced_all))
    block_total = jnp.sum(totals, axis=1)
    before_span = jnp.cumsum(totals, axis=1) - totals
    growth = jnp.exp(block_total)[..., None, None]

    def relay(turn, carried_pair):
        incoming = from_behind(carried_pair[1], "seq", 1)
        return (incoming, growth * incoming + block_end)

    incoming_state, _ = lax.fori_loop(0, lax.axis_size("seq") - 1, relay, (zero_state, block_end))
    entering = (
        entering_local
        + jnp.exp(jnp.moveaxis(before_span, 1, 0))[..., None, None] * incoming_state[None]
    )
    entering_b = entering.astype(jnp.bfloat16)
    inter = jnp.einsum("scqn,cshpn->scqhp", c_spans, entering_b, preferred_element_type=jnp.float32)
    intra = jnp.moveaxis(intra_all, 0, 1)
    mixed = (
        intra
        + jnp.exp(cumulative)[..., None] * inter
        + skip_gain[:, None] * x_spans.astype(jnp.float32)
    )
    mixed = mixed.astype(jnp.bfloat16).reshape(seq_count, length, width)
    return lax.all_to_all(mixed, "head", split_axis=1, concat_axis=2, tiled=True)


def solution(mesh):
    return jax.shard_map(
        local,
        mesh=mesh,
        in_specs=(
            P(None, ("seq", "head"), None),
            P(None, ("seq", "head"), None),
            P(None, ("seq", "head"), None),
            P("head"),
            P("head"),
            P("head"),
            P(None, "head"),
            P("head"),
            P(),
            P(),
        ),
        out_specs=P(None, ("seq", "head"), None),
        check_vma=False,
    )
```

profile of v0, /device:TPU:129, one launch (start us, length us, event | category | flops | bytes accessed | tf_op | source)
XLA Modules:
  0.0 622.9 jit_solution(12799777800667414941)
XLA Ops:
  1.7 7.8 %all-to-all-start.2 = ((bf16[32,2,512]{2,1,0:T(2,128)(2,1)}), bf16[32,2,512]{2,1,0:T(2,128)(2,1)S(1)}, u32[]{:S(2)}, u32[]{:S(2)}) async-start(bf16[32,2,512]{2,1,0:T(2,128)(2,1)} %reshape.173), calls=%async_computation.2 | async-start | bytes 131072 | tf_op jit(solution)/shard_map/all_to_all | solution.py:55
  12.5 5.7 broadcast_in_dim.20
  18.1 13.9 %reshape.171 = bf16[32,2,32768]{2,1,0:T(2,128)(2,1)} reshape(bf16[16384,2,64]{2,1,0:T(2,128)(2,1)} %bitcast.187) | data formatting | bytes 8388608
  32.0 7.4 %all-to-all-start.1 = ((bf16[32,2,32768]{2,1,0:T(2,128)(2,1)}), bf16[32,2,32768]{2,1,0:T(2,128)(2,1)}, u32[]{:S(2)}, u32[]{:S(2)}) async-start(bf16[32,2,32768]{2,1,0:T(2,128)(2,1)} %reshape.171), calls=%async_computation.1 | async-start | bytes 8388608 | tf_op jit(solution)/shard_map/all_to_all | solution.py:56
  39.4 17.8 %copy.77 = bf16[2,64,16384]{1,0,2:T(2,128)(2,1)} copy(bf16[2,64,16384]{2,1,0:T(8,128)(2,1)} %param.16) | data formatting | bytes 8388608 | tf_op args[0]
  57.2 13.9 %reshape.169 = bf16[32,2,32768]{2,1,0:T(2,128)(2,1)} reshape(bf16[16384,2,64]{2,1,0:T(2,128)(2,1)} %bitcast.190) | data formatting | bytes 8388608
  71.1 20.5 %all-to-all-done.1 = bf16[32,2,32768]{2,1,0:T(2,128)(2,1)} async-done(((bf16[32,2,32768]{2,1,0:T(2,128)(2,1)}), bf16[32,2,32768]{2,1,0:T(2,128)(2,1)}, u32[]{:S(2)}, u32[]{:S(2)}) %all-to-all-start.1) | async-done | bytes 4194336 | tf_op jit(solution)/shard_map/all_to_all | solution.py:56
  91.6 7.2 %all-to-all-start = ((bf16[32,2,32768]{2,1,0:T(2,128)(2,1)}), bf16[32,2,32768]{2,1,0:T(2,128)(2,1)}, u32[]{:S(2)}, u32[]{:S(2)}) async-start(bf16[32,2,32768]{2,1,0:T(2,128)(2,1)} %reshape.169), calls=%async_computation | async-start | bytes 8388608 | tf_op jit(solution)/shard_map/all_to_all | solution.py:54
  99.6 9.0 %reduce-window.6 = f32[2,8,8,2,128]{4,2,3,1,0:T(8,128)S(1)} reduce-window(f32[2,8,8,2,128]{4,2,3,1,0:T(8,128)S(1)} %copy.86, f32[]{:T(128)} %constant.75.clone.1), window={size=1x1x1x1x128 pad=0_0x0_0x0_0x0_0x127_0}, to_apply=%region_0.1 | reduce-window | flops 4161536 | bytes 262148 | tf_op jit(solution)/shard_map/reduce-window
  109.4 13.7 %reshape.172 = bf16[16384,2,64]{2,1,0:T(2,128)(2,1)} reshape(bf16[32,2,32768]{2,1,0:T(2,128)(2,1)} %all-to-all-done.1) | data formatting | bytes 8388608
  123.1 18.5 %copy.106 = bf16[2,64,32,512]{3,1,2,0:T(8,128)(2,1)} copy(bf16[2,64,32,512]{1,0,3,2:T(2,128)(2,1)} %bitcast.188) | data formatting | bytes 8388608 | tf_op jit(solution)/shard_map/all_to_all | solution.py:56
  142.4 2.6 collective-permute-start.2
  145.0 6.0 all-to-all-done
  151.0 13.7 %reshape.170 = bf16[16384,2,64]{2,1,0:T(2,128)(2,1)} reshape(bf16[32,2,32768]{2,1,0:T(2,128)(2,1)} %all-to-all-done) | data formatting | bytes 8388608
  164.7 18.5 %copy.78 = bf16[2,64,32,512]{3,1,2,0:T(8,128)(2,1)} copy(bf16[2,64,32,512]{1,0,3,2:T(2,128)(2,1)} %bitcast.189) | data formatting | bytes 8388608 | tf_op jit(solution)/shard_map/all_to_all | solution.py:54
  183.9 2.8 collective-permute-start.1
  186.8 10.9 %multiply_convert_fusion.8 = bf16[2,2048,512]{2,1,0:T(8,128)(2,1)S(1)} fusion(bf16[2,2048,512]{2,1,0:T(8,128)(2,1)} %bitcast.192, bf16[2,3,512]{2,1,0:T(4,128)(2,1)S(1)} %collective-permute-done.2, f32[512]{0:T(512)S(1)} %bitcast.210, f32[512]{0:T(512)S(1)} %bitcast.208, f32[512]{0:T(512)S(1)} %bitcast.209, f32[512]{0:T(512)S(1)} %bitcast.207, ...), kind=kLoop, calls=%fused_computation.44 | loop fusion | flops 54525952 | bytes 8404992 | tf_op jit(solution)/shard_map/convert_element_type | solution.py:26
  200.0 7.0 %multiply_convert_fusion.9 = bf16[2,2048,512]{2,1,0:T(8,128)(2,1)} fusion(bf16[2,2048,512]{2,1,0:T(8,128)(2,1)S(1)} %bitcast.194, bf16[2,3,512]{2,1,0:T(4,128)(2,1)S(1)} %collective-permute-done.1, f32[512]{0:T(512)S(1)} %bitcast.214, f32[512]{0:T(512)S(1)} %bitcast.215, f32[512]{0:T(512)S(1)} %bitcast.213, f32[512]{0:T(512)S(1)} %bitcast.212, ...), kind=kLoop, calls=%fused_computation.45 | loop fusion | flops 54525952 | bytes 8404992 | tf_op jit(solution)/shard_map/convert_element_type | solution.py:26
  207.0 6.3 %copy.79 = bf16[2,2048,512]{1,2,0:T(8,128)(2,1)} copy(bf16[2,2048,512]{2,1,0:T(8,128)(2,1)} %multiply_convert_fusion.9) | data formatting | bytes 8388608 | tf_op jit(solution)/shard_map/convert_element_type | solution.py:26
  213.3 3.7 copy.121
  217.0 3.4 copy.89
  220.4 4.3 broadcast.35.clone
  224.7 85.7 %while.39 = (s32[]{:T(128)}, f32[8,2,256,8,64]{2,4,3,0,1:T(8,128)}, f32[8,2,8,64,256]{4,3,2,1,0:T(8,128)}, s32[8]{0:T(128)S(1)}, bf16[2,8,256,8,64]{2,4,3,0,1:T(...) while((s32[]{:T(128)}, f32[8,2,256,8,64]{2,4,3,0,1:T(8,128)}, ...), condition=%wide.region_3.4_spmd.clone, body=%wide.region_2.3_spmd.clone.sunk | while | flops 342695936 | bytes 5459311 | solution.py:101
  229.1 3.5 fusion.55
  232.9 2.5 fusion.56
  239.9 3.5 fusion.55
  250.5 3.6 fusion.55
  261.2 3.6 fusion.55
  271.9 3.6 fusion.55
  275.8 2.5 fusion.56
  282.7 3.6 fusion.55
  293.4 3.5 fusion.55
  304.1 3.6 fusion.55
  310.4 4.3 broadcast.35
  314.6 20.5 %while.40 = (s32[]{:T(128)}, f32[2,8,64,256]{3,2,1,0:T(8,128)S(1)}, f32[8,2,8,64,256]{4,3,2,1,0:T(8,128)}, f32[8,2,8]{2,0,1:T(8,128)S(1)}, f32[8,2,8,64,256]{4,3,2,1,0:T(8,128)}, /*index=5*/s32[]{:T(128)}, s32[]{:T(128)}) while((s32[]{:T(128)}, f32[2,8,64,256]{3,2,1,0:T(8,128)S(1)}, f32[8,2,8,64,256]{4,3,2,1,0:T(8,128)}, ...), condition=%wide.region_5.6_spmd.clone, body=%wide.region_4.5_spmd.clone.sunk | while | flops 1048579 | bytes 5243808 | solution.py:110
  335.2 173.6 %while.38 = (s32[]{:T(128)}, f32[2,8,64,256]{3,2,1,0:T(8,128)}, f32[2,8,64,256]{3,2,1,0:T(8,128)S(1)}, f32[2,8,1,1]{1,0,3,2:T(2,128)S(1)}, f32[2,8,64,256]{3,2,1,0:T(8,128)S(1)}, /*index=5*/s32[]{:T(128)}) while((s32[]{:T(128)}, f32[2,8,64,256]{3,2,1,0:T(8,128)}, f32[2,8,64,256]{3,2,1,0:T(8,128)S(1)}, f32[2,8,1,1]{1,0,3,2:T(2,128)S(1)}, ...), condition=%wide.region_9.10_spmd, body=%wide.region_8.9_spmd.sunk | while | flops 524290 | bytes 11534537 | solution.py:119
  335.2 2.6 collective-permute-start
  337.9 23.9 %collective-permute-done = f32[2,8,64,256]{3,2,1,0:T(8,128)S(1)} collective-permute-done((f32[2,8,64,256]{3,2,1,0:T(8,128)S(1)}, f32[2,8,64,256]{3,2,1,0:T(8,128)S(1)}, u32[]{:S(2)}, u32[]{:S(2)}) %collective-permute-start) | collective-permute-done | bytes 1048608 | tf_op jit(solution)/shard_map/while/body/eval_jaxpr/ppermute | solution.py:16
  364.7 23.7 %collective-permute-done = f32[2,8,64,256]{3,2,1,0:T(8,128)S(1)} collective-permute-done((f32[2,8,64,256]{3,2,1,0:T(8,128)S(1)}, f32[2,8,64,256]{3,2,1,0:T(8,128)S(1)}, u32[]{:S(2)}, u32[]{:S(2)}) %collective-permute-start) | collective-permute-done | bytes 1048608 | tf_op jit(solution)/shard_map/while/body/eval_jaxpr/ppermute | solution.py:16
  391.4 22.8 %collective-permute-done = f32[2,8,64,256]{3,2,1,0:T(8,128)S(1)} collective-permute-done((f32[2,8,64,256]{3,2,1,0:T(8,128)S(1)}, f32[2,8,64,256]{3,2,1,0:T(8,128)S(1)}, u32[]{:S(2)}, u32[]{:S(2)}) %collective-permute-start) | collective-permute-done | bytes 1048608 | tf_op jit(solution)/shard_map/while/body/eval_jaxpr/ppermute | solution.py:16
  417.1 21.9 %collective-permute-done = f32[2,8,64,256]{3,2,1,0:T(8,128)S(1)} collective-permute-done((f32[2,8,64,256]{3,2,1,0:T(8,128)S(1)}, f32[2,8,64,256]{3,2,1,0:T(8,128)S(1)}, u32[]{:S(2)}, u32[]{:S(2)}) %collective-permute-start) | collective-permute-done | bytes 1048608 | tf_op jit(solution)/shard_map/while/body/eval_jaxpr/ppermute | solution.py:16
  441.9 21.0 %collective-permute-done = f32[2,8,64,256]{3,2,1,0:T(8,128)S(1)} collective-permute-done((f32[2,8,64,256]{3,2,1,0:T(8,128)S(1)}, f32[2,8,64,256]{3,2,1,0:T(8,128)S(1)}, u32[]{:S(2)}, u32[]{:S(2)}) %collective-permute-start) | collective-permute-done | bytes 1048608 | tf_op jit(solution)/shard_map/while/body/eval_jaxpr/ppermute | solution.py:16
  465.8 20.1 %collective-permute-done = f32[2,8,64,256]{3,2,1,0:T(8,128)S(1)} collective-permute-done((f32[2,8,64,256]{3,2,1,0:T(8,128)S(1)}, f32[2,8,64,256]{3,2,1,0:T(8,128)S(1)}, u32[]{:S(2)}, u32[]{:S(2)}) %collective-permute-start) | collective-permute-done | bytes 1048608 | tf_op jit(solution)/shard_map/while/body/eval_jaxpr/ppermute | solution.py:16
  488.7 19.1 %collective-permute-done = f32[2,8,64,256]{3,2,1,0:T(8,128)S(1)} collective-permute-done((f32[2,8,64,256]{3,2,1,0:T(8,128)S(1)}, f32[2,8,64,256]{3,2,1,0:T(8,128)S(1)}, u32[]{:S(2)}, u32[]{:S(2)}) %collective-permute-start) | collective-permute-done | bytes 1048608 | tf_op jit(solution)/shard_map/while/body/eval_jaxpr/ppermute | solution.py:16
  508.9 11.4 %fusion.29 = bf16[2,8,256,8,64]{2,4,3,1,0:T(8,128)(2,1)} fusion(f32[8,2,256,8,64]{2,4,3,0,1:T(8,128)} %get-tuple-element.112, bf16[2,8,256,8,64]{2,1,4,3,0:T(8,128)(2,1)} %bitcast.186, f32[8]{0:T(128)S(1)} %copy-done.7, f32[2,8,256,8]{2,3,1,0:T(8,128)S(1)} %get-tuple-element.251, bf16[2,8,256,256,1]{3,2,4,1,0:T(8,128)(2,1)} %bitcast.33, ...), kind=kOutput, calls=%fused_computation.42 | convolution fusion | flops 1092616192 | bytes 28443168 | tf_op jit(solution)/shard_map/scqn,cshpn->scqhp/dot_general | solution.py:125
  520.2 10.9 %copy.107 = bf16[2,8,256,8,64]{4,3,0,2,1:T(8,128)(2,1)} copy(bf16[2,8,256,8,64]{2,4,3,1,0:T(8,128)(2,1)} %fusion.29) | data formatting | bytes 8388608 | tf_op jit(solution)/shard_map/reshape | solution.py:132
  531.2 13.1 %reshape.167 = bf16[2,2048,512]{2,0,1:T(2,128)(2,1)} reshape(bf16[2,8,256,8,64]{4,3,0,2,1:T(8,128)(2,1)} %copy.107) | data formatting | bytes 8388608 | tf_op jit(solution)/shard_map/reshape | solution.py:132
  544.2 75.5 %all_to_all.63 = bf16[2,2048,512]{2,0,1:T(2,128)(2,1)S(1)} all-to-all(bf16[2,2048,512]{2,0,1:T(2,128)(2,1)} %reshape.167), channel_id=1, replica_groups=mesh['seq'=8,'head'=32] {'head'}, dimensions={1} | all-to-all | bytes 8388608 | tf_op jit(solution)/shard_map/all_to_all | solution.py:133
  (218 shorter events, 88.6 us)
Async XLA Ops:
  1.7 30.3 %all-to-all-start.2 = ((bf16[32,2,512]{2,1,0:T(2,128)(2,1)}), bf16[32,2,512]{2,1,0:T(2,128)(2,1)S(1)}, u32[]{:S(2)}, u32[]{:S(2)}) async-start(bf16[32,2,512]{2,1,0:T(2,128)(2,1)} %reshape.173), calls=%async_computation.2 | async-start | bytes 131072 | tf_op jit(solution)/shard_map/all_to_all | solution.py:55
  32.0 59.7 %all-to-all-start.1 = ((bf16[32,2,32768]{2,1,0:T(2,128)(2,1)}), bf16[32,2,32768]{2,1,0:T(2,128)(2,1)}, u32[]{:S(2)}, u32[]{:S(2)}) async-start(bf16[32,2,32768]{2,1,0:T(2,128)(2,1)} %reshape.171), calls=%async_computation.1 | async-start | bytes 8388608 | tf_op jit(solution)/shard_map/all_to_all | solution.py:56
  57.2 41.7 %copy-start.3 = (bf16[4,4096]{1,0:T(4,128)(2,1)S(1)}, bf16[4,4096]{1,0:T(4,128)(2,1)}, u32[]{:S(2)}) copy-start(bf16[4,4096]{1,0:T(4,128)(2,1)} %param.24) | copy-start | bytes 98308
  57.2 41.7 %copy-start.4 = (f32[4096]{0:T(1024)S(1)}, f32[4096]{0:T(1024)}, u32[]{:S(2)}) copy-start(f32[4096]{0:T(1024)} %param.25) | copy-start | bytes 49156
  57.2 41.8 %copy-start.5 = (bf16[4,512]{1,0:T(4,128)(2,1)S(1)}, bf16[4,512]{1,0:T(4,128)(2,1)}, u32[]{:S(2)}) copy-start(bf16[4,512]{1,0:T(4,128)(2,1)} %param.22) | copy-start | bytes 12292
  57.2 42.2 %copy-start.8 = (f32[8]{0:T(128)S(1)}, f32[8]{0:T(128)}, u32[]{:S(2)}) copy-start(f32[8]{0:T(128)} %param.20) | copy-start | bytes 100
  57.2 42.2 %copy-start.9 = (f32[8]{0:T(128)S(1)}, f32[8]{0:T(128)}, u32[]{:S(2)}) copy-start(f32[8]{0:T(128)} %param.19) | copy-start | bytes 100
  91.6 59.4 %all-to-all-start = ((bf16[32,2,32768]{2,1,0:T(2,128)(2,1)}), bf16[32,2,32768]{2,1,0:T(2,128)(2,1)}, u32[]{:S(2)}, u32[]{:S(2)}) async-start(bf16[32,2,32768]{2,1,0:T(2,128)(2,1)} %reshape.169), calls=%async_computation | async-start | bytes 8388608 | tf_op jit(solution)/shard_map/all_to_all | solution.py:54
  142.4 44.4 %collective-permute-start.2 = (bf16[2,3,512]{2,1,0:T(4,128)(2,1)S(1)}, bf16[2,3,512]{2,1,0:T(4,128)(2,1)S(1)}, u32[]{:S(2)}, u32[]{:S(2)}) collective-permute-start(bf16[2,3,512]{2,1,0:T(4,128)(2,1)S(1)} %slice.98), channel_id=1, source_target_pairs={{0,32},{32,64},{64,96},{96,128},{128,160},{160,192},{192,224},{1,3... | collective-permute-start | bytes 18440 | tf_op jit(solution)/shard_map/ppermute | solution.py:16
  183.9 16.1 %collective-permute-start.1 = (bf16[2,3,512]{2,1,0:T(4,128)(2,1)S(1)}, bf16[2,3,512]{2,1,0:T(4,128)(2,1)S(1)}, u32[]{:S(2)}, u32[]{:S(2)}) collective-permute-start(bf16[2,3,512]{2,1,0:T(4,128)(2,1)S(1)} %slice.93), channel_id=1, source_target_pairs={{0,32},{32,64},{64,96},{96,128},{128,160},{160,192},{192,224},{1,3... | collective-permute-start | bytes 18440 | tf_op jit(solution)/shard_map/ppermute | solution.py:16
  186.7 13.2 %copy-start.2 = (bf16[2,64,32,512]{3,1,2,0:T(8,128)(2,1)S(1)}, bf16[2,64,32,512]{3,1,2,0:T(8,128)(2,1)}, u32[]{:S(2)}) copy-start(bf16[2,64,32,512]{3,1,2,0:T(8,128)(2,1)} %copy.78) | copy-start | bytes 12582916
  186.8 13.2 %copy-start.6 = (f32[512]{0:T(512)S(1)}, f32[512]{0:T(512)}, u32[]{:S(2)}) copy-start(f32[512]{0:T(512)} %param.23) | copy-start | bytes 6148
  217.0 7.7 %copy-start = (bf16[128,8,8,256]{3,2,1,0:T(8,128)(2,1)}, bf16[128,8,8,256]{3,2,1,0:T(8,128)(2,1)S(1)}, u32[]{:S(2)}) copy-start(bf16[128,8,8,256]{3,2,1,0:T(8,128)(2,1)S(1)} %copy.121) | copy-start | bytes 12582916
  335.2 173.7 %copy-start.7 = (f32[8]{0:T(128)S(1)}, f32[8]{0:T(128)}, u32[]{:S(2)}) copy-start(f32[8]{0:T(128)} %param.21) | copy-start | bytes 100
  335.2 26.6 %collective-permute-start = (f32[2,8,64,256]{3,2,1,0:T(8,128)S(1)}, f32[2,8,64,256]{3,2,1,0:T(8,128)S(1)}, u32[]{:S(2)}, u32[]{:S(2)}) collective-permute-start(f32[2,8,64,256]{3,2,1,0:T(8,128)S(1)} %get-tuple-element.445), channel_id=1, source_target_pairs={{0,32},{32,64},{64,96},{96,128},{128,160},{160,192},{192,224},{1,3... | collective-permute-start | bytes 3145736 | tf_op jit(solution)/shard_map/while/body/eval_jaxpr/ppermute | solution.py:16
  361.8 1.0 copy-start.1
  362.8 25.7 %collective-permute-start = (f32[2,8,64,256]{3,2,1,0:T(8,128)S(1)}, f32[2,8,64,256]{3,2,1,0:T(8,128)S(1)}, u32[]{:S(2)}, u32[]{:S(2)}) collective-permute-start(f32[2,8,64,256]{3,2,1,0:T(8,128)S(1)} %get-tuple-element.445), channel_id=1, source_target_pairs={{0,32},{32,64},{64,96},{96,128},{128,160},{160,192},{192,224},{1,3... | collective-permute-start | bytes 3145736 | tf_op jit(solution)/shard_map/while/body/eval_jaxpr/ppermute | solution.py:16
  388.5 1.0 copy-start.1
  389.5 24.7 %collective-permute-start = (f32[2,8,64,256]{3,2,1,0:T(8,128)S(1)}, f32[2,8,64,256]{3,2,1,0:T(8,128)S(1)}, u32[]{:S(2)}, u32[]{:S(2)}) collective-permute-start(f32[2,8,64,256]{3,2,1,0:T(8,128)S(1)} %get-tuple-element.445), channel_id=1, source_target_pairs={{0,32},{32,64},{64,96},{96,128},{128,160},{160,192},{192,224},{1,3... | collective-permute-start | bytes 3145736 | tf_op jit(solution)/shard_map/while/body/eval_jaxpr/ppermute | solution.py:16
  414.2 1.0 copy-start.1
  415.2 23.8 %collective-permute-start = (f32[2,8,64,256]{3,2,1,0:T(8,128)S(1)}, f32[2,8,64,256]{3,2,1,0:T(8,128)S(1)}, u32[]{:S(2)}, u32[]{:S(2)}) collective-permute-start(f32[2,8,64,256]{3,2,1,0:T(8,128)S(1)} %get-tuple-element.445), channel_id=1, source_target_pairs={{0,32},{32,64},{64,96},{96,128},{128,160},{160,192},{192,224},{1,3... | collective-permute-start | bytes 3145736 | tf_op jit(solution)/shard_map/while/body/eval_jaxpr/ppermute | solution.py:16
  439.0 1.0 copy-start.1
  440.0 22.9 %collective-permute-start = (f32[2,8,64,256]{3,2,1,0:T(8,128)S(1)}, f32[2,8,64,256]{3,2,1,0:T(8,128)S(1)}, u32[]{:S(2)}, u32[]{:S(2)}) collective-permute-start(f32[2,8,64,256]{3,2,1,0:T(8,128)S(1)} %get-tuple-element.445), channel_id=1, source_target_pairs={{0,32},{32,64},{64,96},{96,128},{128,160},{160,192},{192,224},{1,3... | collective-permute-start | bytes 3145736 | tf_op jit(solution)/shard_map/while/body/eval_jaxpr/ppermute | solution.py:16
  462.9 1.0 copy-start.1
  463.9 22.0 %collective-permute-start = (f32[2,8,64,256]{3,2,1,0:T(8,128)S(1)}, f32[2,8,64,256]{3,2,1,0:T(8,128)S(1)}, u32[]{:S(2)}, u32[]{:S(2)}) collective-permute-start(f32[2,8,64,256]{3,2,1,0:T(8,128)S(1)} %get-tuple-element.445), channel_id=1, source_target_pairs={{0,32},{32,64},{64,96},{96,128},{128,160},{160,192},{192,224},{1,3... | collective-permute-start | bytes 3145736 | tf_op jit(solution)/shard_map/while/body/eval_jaxpr/ppermute | solution.py:16
  485.8 1.0 copy-start.1
  486.8 21.1 %collective-permute-start = (f32[2,8,64,256]{3,2,1,0:T(8,128)S(1)}, f32[2,8,64,256]{3,2,1,0:T(8,128)S(1)}, u32[]{:S(2)}, u32[]{:S(2)}) collective-permute-start(f32[2,8,64,256]{3,2,1,0:T(8,128)S(1)} %get-tuple-element.445), channel_id=1, source_target_pairs={{0,32},{32,64},{64,96},{96,128},{128,160},{160,192},{192,224},{1,3... | collective-permute-start | bytes 3145736 | tf_op jit(solution)/shard_map/while/body/eval_jaxpr/ppermute | solution.py:16
  507.9 1.0 copy-start.1
where the time goes:
time: 628 us; the launch traced here: 623 us
  local copies, waits for them, and re-layouts  190 us (30%)
  waiting for transfers between devices  179 us (29%)
  blocking collectives  75.5 us (12%)
  matrix products  69.6 us (11%)
  other arithmetic  50.7 us (8%)
  starting transfers between devices  41.9 us (7%)
  loops' own time  15.6 us (2%)
    ppermute x9, waiting for transfers between devices, from_behind(): return lax.ppermute(array, axis, pairs)  153 us
    unnamed x31, local copies, waits for them, and re-layouts  83.4 us
    all_to_all x1, blocking collectives, local(): lax.all_to_all(mixed, 'head', split_axis=1, concat_axis=2, tiled=True)  75.5 us
    dot_general x8, matrix products, span_work(): jnp.einsum('shtk,skhp->sthp', weights, x_here, preferred_element_type=jnp...  28.4 us
    reshape x2, local copies, waits for them, and re-layouts, local(): mixed = mixed.astype(jnp.bfloat16).reshape(seq_count, length, width)  24 us
    all_to_all x1, waiting for transfers between devices, local(): lax.all_to_all(sent_maps, 'head', split_axis=2, concat_axis=1, tiled=True)  20.5 us
    ppermute x9, starting transfers between devices, from_behind(): return lax.ppermute(array, axis, pairs)  19.5 us
    dot_general x8, matrix products, span_work(): jnp.einsum('skhp,skn->shpn', carried, b_here, preferred_element_type=jnp....  19.4 us
  transfers between devices with their start and end apart: 12, of which 9 were waited for; matrix products, arithmetic and copies ran while one was open for 23% of the time, Pallas kernels for 0%

commit v1 on v0

--- a/solution.py
+++ b/solution.py
@@ -50,8 +50,16 @@
         grouped[:, :, :, None], (seq_count, row_count, GROUPS, repeats, 2, STATE)
     )
     sent_maps = spread.reshape(seq_count, row_count, head_count * 2 * STATE)
+
+    def remake_sectors_on_mesh(vals):
+        n_now = lax.axis_size("head")
+        fresh = jnp.split(vals, n_now, axis=2)
+        last = jnp.stack(fresh)
+        placed = lax.all_to_all(last, "head", 0, 0)
+        return jnp.concatenate(placed, axis=1)
+
     local_x, local_step, local_maps = (
-        lax.all_to_all(projected, "head", split_axis=2, concat_axis=1, tiled=True),
+        remake_sectors_on_mesh(projected),
         lax.all_to_all(step_raw, "head", split_axis=2, concat_axis=1, tiled=True),
         lax.all_to_all(sent_maps, "head", split_axis=2, concat_axis=1, tiled=True),
     )

time: 628 us -> 613 us (0.976)
  local copies, waits for them, and re-layouts: 190 us -> 177 us
    all_to_all x1, local copies, waits for them, and re-layouts: 18.5 us -> 2.82 us  [remake_sectors_on_mesh(): placed = lax.all_to_all(last, 'head', 0, 0)]
    unnamed x31 -> x61, local copies, waits for them, and re-layouts: 83.4 us -> 85.5 us
  transfers between devices with their start and end apart: 12 -> 12, of which waited for: 9 -> 9; matrix products, arithmetic and copies ran while one was open for 23% -> 21% of each run, Pallas kernels for 0% -> 0%
where the time goes in v1:
time: 613 us; the launch traced here: 609 us
  waiting for transfers between devices  183 us (30%)
  local copies, waits for them, and re-layouts  177 us (29%)
  blocking collectives  75.6 us (12%)
  matrix products  69.5 us (11%)
  other arithmetic  45.9 us (7%)
  starting transfers between devices  41.9 us (7%)
  loops' own time  15.7 us (3%)
    ppermute x9, waiting for transfers between devices, from_behind(): return lax.ppermute(array, axis, pairs)  153 us
    unnamed x61, local copies, waits for them, and re-layouts  85.5 us
    all_to_all x1, blocking collectives, local(): lax.all_to_all(mixed, 'head', split_axis=1, concat_axis=2, tiled=True)  75.6 us
    dot_general x8, matrix products, span_work(): jnp.einsum('shtk,skhp->sthp', weights, x_here, preferred_element_type=jnp...  28.4 us
    reshape x2, local copies, waits for them, and re-layouts, local(): mixed = mixed.astype(jnp.bfloat16).reshape(seq_count, length, width)  24 us
    all_to_all x1, waiting for transfers between devices, local(): lax.all_to_all(sent_maps, 'head', split_axis=2, concat_axis=1, tiled=True)  24 us
    ppermute x9, starting transfers between devices, from_behind(): return lax.ppermute(array, axis, pairs)  19.6 us
    dot_general x8, matrix products, span_work(): jnp.einsum('skhp,skn->shpn', carried, b_here, preferred_element_type=jnp....  19.4 us
  transfers between devices with their start and end apart: 12, of which 9 were waited for; matrix products, arithmetic and copies ran while one was open for 21% of the time, Pallas kernels for 0%

profile of v1, /device:TPU:129, one launch (start us, length us, event | category | flops | bytes accessed | tf_op | source)
XLA Modules:
  0.0 608.7 jit_solution(14639581643695998523)
XLA Ops:
  1.8 7.8 %all-to-all-start.2 = ((bf16[32,2,512]{2,1,0:T(2,128)(2,1)}), bf16[32,2,512]{2,1,0:T(2,128)(2,1)S(1)}, u32[]{:S(2)}, u32[]{:S(2)}) async-start(bf16[32,2,512]{2,1,0:T(2,128)(2,1)} %reshape.179), calls=%async_computation.2 | async-start | bytes 131072 | tf_op jit(solution)/shard_map/all_to_all | solution.py:63
  33.3 5.6 broadcast_in_dim.20
  38.9 13.9 %reshape.177 = bf16[32,2,32768]{2,1,0:T(2,128)(2,1)} reshape(bf16[16384,2,64]{2,1,0:T(2,128)(2,1)} %bitcast.248) | data formatting | bytes 8388608
  52.8 7.4 %all-to-all-start.1 = ((bf16[32,2,32768]{2,1,0:T(2,128)(2,1)}), bf16[32,2,32768]{2,1,0:T(2,128)(2,1)}, u32[]{:S(2)}, u32[]{:S(2)}) async-start(bf16[32,2,32768]{2,1,0:T(2,128)(2,1)} %reshape.177), calls=%async_computation.1 | async-start | bytes 8388608 | tf_op jit(solution)/shard_map/all_to_all | solution.py:64
  88.5 24.0 %all-to-all-done.1 = bf16[32,2,32768]{2,1,0:T(2,128)(2,1)} async-done(((bf16[32,2,32768]{2,1,0:T(2,128)(2,1)}), bf16[32,2,32768]{2,1,0:T(2,128)(2,1)}, u32[]{:S(2)}, u32[]{:S(2)}) %all-to-all-start.1) | async-done | bytes 4194336 | tf_op jit(solution)/shard_map/all_to_all | solution.py:64
  112.5 7.2 %all-to-all-start = ((bf16[32,2,64,512]{3,2,1,0:T(8,128)(2,1)}), bf16[32,2,64,512]{3,2,1,0:T(8,128)(2,1)}, u32[]{:S(2)}, u32[]{:S(2)}) async-start(bf16[32,2,64,512]{3,2,1,0:T(8,128)(2,1)} %bitcast_dynamic-update-slice_fusion.1), calls=%async_computation | async-start | bytes 8388608 | tf_op jit(solution)/shard_map/all_to_all | solution.py:58
  120.4 9.0 %reduce-window.6 = f32[2,8,8,2,128]{4,2,3,1,0:T(8,128)S(1)} reduce-window(f32[2,8,8,2,128]{4,2,3,1,0:T(8,128)S(1)} %copy.83, f32[]{:T(128)} %constant.75.clone.1), window={size=1x1x1x1x128 pad=0_0x0_0x0_0x0_0x127_0}, to_apply=%region_0.1 | reduce-window | flops 4161536 | bytes 262148 | tf_op jit(solution)/shard_map/reduce-window
  130.3 13.6 %reshape.178 = bf16[16384,2,64]{2,1,0:T(2,128)(2,1)} reshape(bf16[32,2,32768]{2,1,0:T(2,128)(2,1)} %all-to-all-done.1) | data formatting | bytes 8388608
  143.9 18.5 %copy.103 = bf16[2,64,32,512]{3,1,2,0:T(8,128)(2,1)} copy(bf16[2,64,32,512]{1,0,3,2:T(2,128)(2,1)} %bitcast.249) | data formatting | bytes 8388608 | tf_op jit(solution)/shard_map/all_to_all | solution.py:64
  163.2 2.6 collective-permute-start.2
  165.8 6.0 all-to-all-done
  171.9 2.8 copy.75
  174.7 2.8 collective-permute-start.1
  177.6 6.1 %multiply_convert_fusion.8 = bf16[2,2048,512]{2,1,0:T(8,128)(2,1)S(1)} fusion(bf16[2,2048,512]{2,1,0:T(8,128)(2,1)S(1)} %bitcast.251, bf16[2,3,512]{2,1,0:T(4,128)(2,1)S(1)} %collective-permute-done.2, f32[512]{0:T(512)S(1)} %bitcast.269, f32[512]{0:T(512)S(1)} %bitcast.267, f32[512]{0:T(512)S(1)} %bitcast.268, f32[512]{0:T(512)S(1)} %bitcast.266, ...), kind=kLoop, calls=%fused_computation.44 | loop fusion | flops 54525952 | bytes 8404992 | tf_op jit(solution)/shard_map/convert_element_type | solution.py:26
  186.0 7.0 %multiply_convert_fusion.9 = bf16[2,2048,512]{2,1,0:T(8,128)(2,1)} fusion(bf16[2,2048,512]{2,1,0:T(8,128)(2,1)S(1)} %bitcast.253, bf16[2,3,512]{2,1,0:T(4,128)(2,1)S(1)} %collective-permute-done.1, f32[512]{0:T(512)S(1)} %bitcast.273, f32[512]{0:T(512)S(1)} %bitcast.274, f32[512]{0:T(512)S(1)} %bitcast.272, f32[512]{0:T(512)S(1)} %bitcast.271, ...), kind=kLoop, calls=%fused_computation.45 | loop fusion | flops 54525952 | bytes 8404992 | tf_op jit(solution)/shard_map/convert_element_type | solution.py:26
  193.1 6.3 %copy.76 = bf16[2,2048,512]{1,2,0:T(8,128)(2,1)} copy(bf16[2,2048,512]{2,1,0:T(8,128)(2,1)} %multiply_convert_fusion.9) | data formatting | bytes 8388608 | tf_op jit(solution)/shard_map/convert_element_type | solution.py:26
  199.4 3.7 copy.118
  203.0 3.4 copy.86
  206.4 4.3 broadcast.35.clone
  210.7 85.3 %while.39 = (s32[]{:T(128)}, f32[8,2,256,8,64]{2,4,3,0,1:T(8,128)}, f32[8,2,8,64,256]{4,3,2,1,0:T(8,128)}, s32[8]{0:T(128)S(1)}, bf16[2,8,256,8,64]{2,4,3,0,1:T(...) while((s32[]{:T(128)}, f32[8,2,256,8,64]{2,4,3,0,1:T(8,128)}, ...), condition=%wide.region_3.4_spmd.clone, body=%wide.region_2.3_spmd.clone.sunk | while | flops 342695936 | bytes 5459311 | solution.py:109
  215.1 3.5 fusion.55
  219.0 2.5 fusion.56
  225.9 3.5 fusion.55
  236.5 3.6 fusion.55
  240.3 2.4 fusion.56
  247.1 3.5 fusion.55
  251.0 2.4 fusion.56
  257.8 3.6 fusion.55
  261.7 2.5 fusion.56
  268.5 3.5 fusion.55
  279.2 3.5 fusion.55
  289.8 3.6 fusion.55
  296.1 4.3 broadcast.35
  300.4 20.5 %while.40 = (s32[]{:T(128)}, f32[2,8,64,256]{3,2,1,0:T(8,128)S(1)}, f32[8,2,8,64,256]{4,3,2,1,0:T(8,128)}, f32[8,2,8]{2,0,1:T(8,128)S(1)}, f32[8,2,8,64,256]{4,3,2,1,0:T(8,128)}, /*index=5*/s32[]{:T(128)}, s32[]{:T(128)}) while((s32[]{:T(128)}, f32[2,8,64,256]{3,2,1,0:T(8,128)S(1)}, f32[8,2,8,64,256]{4,3,2,1,0:T(8,128)}, ...), condition=%wide.region_5.6_spmd.clone, body=%wide.region_4.5_spmd.clone.sunk | while | flops 1048579 | bytes 5243808 | solution.py:118
  321.0 173.6 %while.38 = (s32[]{:T(128)}, f32[2,8,64,256]{3,2,1,0:T(8,128)}, f32[2,8,64,256]{3,2,1,0:T(8,128)S(1)}, f32[2,8,1,1]{1,0,3,2:T(2,128)S(1)}, f32[2,8,64,256]{3,2,1,0:T(8,128)S(1)}, /*index=5*/s32[]{:T(128)}) while((s32[]{:T(128)}, f32[2,8,64,256]{3,2,1,0:T(8,128)}, f32[2,8,64,256]{3,2,1,0:T(8,128)S(1)}, f32[2,8,1,1]{1,0,3,2:T(2,128)S(1)}, ...), condition=%wide.region_9.10_spmd, body=%wide.region_8.9_spmd.sunk | while | flops 524290 | bytes 11534537 | solution.py:127
  321.0 2.6 collective-permute-start
  323.6 23.9 %collective-permute-done = f32[2,8,64,256]{3,2,1,0:T(8,128)S(1)} collective-permute-done((f32[2,8,64,256]{3,2,1,0:T(8,128)S(1)}, f32[2,8,64,256]{3,2,1,0:T(8,128)S(1)}, u32[]{:S(2)}, u32[]{:S(2)}) %collective-permute-start) | collective-permute-done | bytes 1048608 | tf_op jit(solution)/shard_map/while/body/eval_jaxpr/ppermute | solution.py:16
  350.5 23.7 %collective-permute-done = f32[2,8,64,256]{3,2,1,0:T(8,128)S(1)} collective-permute-done((f32[2,8,64,256]{3,2,1,0:T(8,128)S(1)}, f32[2,8,64,256]{3,2,1,0:T(8,128)S(1)}, u32[]{:S(2)}, u32[]{:S(2)}) %collective-permute-start) | collective-permute-done | bytes 1048608 | tf_op jit(solution)/shard_map/while/body/eval_jaxpr/ppermute | solution.py:16
  377.1 22.8 %collective-permute-done = f32[2,8,64,256]{3,2,1,0:T(8,128)S(1)} collective-permute-done((f32[2,8,64,256]{3,2,1,0:T(8,128)S(1)}, f32[2,8,64,256]{3,2,1,0:T(8,128)S(1)}, u32[]{:S(2)}, u32[]{:S(2)}) %collective-permute-start) | collective-permute-done | bytes 1048608 | tf_op jit(solution)/shard_map/while/body/eval_jaxpr/ppermute | solution.py:16
  402.8 21.9 %collective-permute-done = f32[2,8,64,256]{3,2,1,0:T(8,128)S(1)} collective-permute-done((f32[2,8,64,256]{3,2,1,0:T(8,128)S(1)}, f32[2,8,64,256]{3,2,1,0:T(8,128)S(1)}, u32[]{:S(2)}, u32[]{:S(2)}) %collective-permute-start) | collective-permute-done | bytes 1048608 | tf_op jit(solution)/shard_map/while/body/eval_jaxpr/ppermute | solution.py:16
  427.6 21.0 %collective-permute-done = f32[2,8,64,256]{3,2,1,0:T(8,128)S(1)} collective-permute-done((f32[2,8,64,256]{3,2,1,0:T(8,128)S(1)}, f32[2,8,64,256]{3,2,1,0:T(8,128)S(1)}, u32[]{:S(2)}, u32[]{:S(2)}) %collective-permute-start) | collective-permute-done | bytes 1048608 | tf_op jit(solution)/shard_map/while/body/eval_jaxpr/ppermute | solution.py:16
  451.5 20.1 %collective-permute-done = f32[2,8,64,256]{3,2,1,0:T(8,128)S(1)} collective-permute-done((f32[2,8,64,256]{3,2,1,0:T(8,128)S(1)}, f32[2,8,64,256]{3,2,1,0:T(8,128)S(1)}, u32[]{:S(2)}, u32[]{:S(2)}) %collective-permute-start) | collective-permute-done | bytes 1048608 | tf_op jit(solution)/shard_map/while/body/eval_jaxpr/ppermute | solution.py:16
  474.5 19.1 %collective-permute-done = f32[2,8,64,256]{3,2,1,0:T(8,128)S(1)} collective-permute-done((f32[2,8,64,256]{3,2,1,0:T(8,128)S(1)}, f32[2,8,64,256]{3,2,1,0:T(8,128)S(1)}, u32[]{:S(2)}, u32[]{:S(2)}) %collective-permute-start) | collective-permute-done | bytes 1048608 | tf_op jit(solution)/shard_map/while/body/eval_jaxpr/ppermute | solution.py:16
  494.6 11.4 %fusion.29 = bf16[2,8,256,8,64]{2,4,3,1,0:T(8,128)(2,1)} fusion(f32[8,2,256,8,64]{2,4,3,0,1:T(8,128)} %get-tuple-element.112, bf16[2,8,256,8,64]{2,1,4,3,0:T(8,128)(2,1)} %bitcast.247, f32[8]{0:T(128)S(1)} %copy-done.8, f32[2,8,256,8]{2,3,1,0:T(8,128)S(1)} %get-tuple-element.251, bf16[2,8,256,256,1]{3,2,4,1,0:T(8,128)(2,1)} %bitcast.64, ...), kind=kOutput, calls=%fused_computation.42 | convolution fusion | flops 1092616192 | bytes 28443168 | tf_op jit(solution)/shard_map/scqn,cshpn->scqhp/dot_general | solution.py:133
  506.0 10.9 %copy.104 = bf16[2,8,256,8,64]{4,3,0,2,1:T(8,128)(2,1)} copy(bf16[2,8,256,8,64]{2,4,3,1,0:T(8,128)(2,1)} %fusion.29) | data formatting | bytes 8388608 | tf_op jit(solution)/shard_map/reshape | solution.py:140
  516.9 13.1 %reshape.175 = bf16[2,2048,512]{2,0,1:T(2,128)(2,1)} reshape(bf16[2,8,256,8,64]{4,3,0,2,1:T(8,128)(2,1)} %copy.104) | data formatting | bytes 8388608 | tf_op jit(solution)/shard_map/reshape | solution.py:140
  530.0 75.6 %all_to_all.50 = bf16[2,2048,512]{2,0,1:T(2,128)(2,1)S(1)} all-to-all(bf16[2,2048,512]{2,0,1:T(2,128)(2,1)} %reshape.175), channel_id=1, replica_groups=mesh['seq'=8,'head'=32] {'head'}, dimensions={1} | all-to-all | bytes 8388608 | tf_op jit(solution)/shard_map/all_to_all | solution.py:141
  606.2 2.5 copy.117
  (249 shorter events, 129.2 us)
Async XLA Ops:
  0.0 31.5 %copy-start.3 = (bf16[2,64,4096]{2,1,0:T(8,128)(2,1)S(1)}, bf16[2,64,4096]{2,1,0:T(8,128)(2,1)}, u32[]{:S(2)}) copy-start(bf16[2,64,4096]{2,1,0:T(8,128)(2,1)} %param.17) | copy-start | bytes 3145732
  1.8 51.0 %all-to-all-start.2 = ((bf16[32,2,512]{2,1,0:T(2,128)(2,1)}), bf16[32,2,512]{2,1,0:T(2,128)(2,1)S(1)}, u32[]{:S(2)}, u32[]{:S(2)}) async-start(bf16[32,2,512]{2,1,0:T(2,128)(2,1)} %reshape.179), calls=%async_computation.2 | async-start | bytes 131072 | tf_op jit(solution)/shard_map/all_to_all | solution.py:63
  52.8 59.7 %all-to-all-start.1 = ((bf16[32,2,32768]{2,1,0:T(2,128)(2,1)}), bf16[32,2,32768]{2,1,0:T(2,128)(2,1)}, u32[]{:S(2)}, u32[]{:S(2)}) async-start(bf16[32,2,32768]{2,1,0:T(2,128)(2,1)} %reshape.177), calls=%async_computation.1 | async-start | bytes 8388608 | tf_op jit(solution)/shard_map/all_to_all | solution.py:64
  88.5 31.2 %copy-start.4 = (bf16[4,4096]{1,0:T(4,128)(2,1)S(1)}, bf16[4,4096]{1,0:T(4,128)(2,1)}, u32[]{:S(2)}) copy-start(bf16[4,4096]{1,0:T(4,128)(2,1)} %param.24) | copy-start | bytes 98308
  88.5 31.3 %copy-start.5 = (f32[4096]{0:T(1024)S(1)}, f32[4096]{0:T(1024)}, u32[]{:S(2)}) copy-start(f32[4096]{0:T(1024)} %param.25) | copy-start | bytes 49156
  88.5 31.3 %copy-start.6 = (bf16[4,512]{1,0:T(4,128)(2,1)S(1)}, bf16[4,512]{1,0:T(4,128)(2,1)}, u32[]{:S(2)}) copy-start(bf16[4,512]{1,0:T(4,128)(2,1)} %param.22) | copy-start | bytes 12292
  88.5 31.7 %copy-start.9 = (f32[8]{0:T(128)S(1)}, f32[8]{0:T(128)}, u32[]{:S(2)}) copy-start(f32[8]{0:T(128)} %param.20) | copy-start | bytes 100
  88.5 31.7 %copy-start.10 = (f32[8]{0:T(128)S(1)}, f32[8]{0:T(128)}, u32[]{:S(2)}) copy-start(f32[8]{0:T(128)} %param.19) | copy-start | bytes 100
  112.5 59.4 %all-to-all-start = ((bf16[32,2,64,512]{3,2,1,0:T(8,128)(2,1)}), bf16[32,2,64,512]{3,2,1,0:T(8,128)(2,1)}, u32[]{:S(2)}, u32[]{:S(2)}) async-start(bf16[32,2,64,512]{3,2,1,0:T(8,128)(2,1)} %bitcast_dynamic-update-slice_fusion.1), calls=%async_computation | async-start | bytes 8388608 | tf_op jit(solution)/shard_map/all_to_all | solution.py:58
  163.2 14.4 %collective-permute-start.2 = (bf16[2,3,512]{2,1,0:T(4,128)(2,1)S(1)}, bf16[2,3,512]{2,1,0:T(4,128)(2,1)S(1)}, u32[]{:S(2)}, u32[]{:S(2)}) collective-permute-start(bf16[2,3,512]{2,1,0:T(4,128)(2,1)S(1)} %slice.98), channel_id=1, source_target_pairs={{0,32},{32,64},{64,96},{96,128},{128,160},{160,192},{192,224},{1,3... | collective-permute-start | bytes 18440 | tf_op jit(solution)/shard_map/ppermute | solution.py:16
  171.9 5.7 copy-start.2
  174.7 11.3 %collective-permute-start.1 = (bf16[2,3,512]{2,1,0:T(4,128)(2,1)S(1)}, bf16[2,3,512]{2,1,0:T(4,128)(2,1)S(1)}, u32[]{:S(2)}, u32[]{:S(2)}) collective-permute-start(bf16[2,3,512]{2,1,0:T(4,128)(2,1)S(1)} %slice.93), channel_id=1, source_target_pairs={{0,32},{32,64},{64,96},{96,128},{128,160},{160,192},{192,224},{1,3... | collective-permute-start | bytes 18440 | tf_op jit(solution)/shard_map/ppermute | solution.py:16
  183.7 2.3 copy-start.7
  203.0 3.4 copy-start
  320.9 173.6 %copy-start.8 = (f32[8]{0:T(128)S(1)}, f32[8]{0:T(128)}, u32[]{:S(2)}) copy-start(f32[8]{0:T(128)} %param.21) | copy-start | bytes 100
  321.0 26.6 %collective-permute-start = (f32[2,8,64,256]{3,2,1,0:T(8,128)S(1)}, f32[2,8,64,256]{3,2,1,0:T(8,128)S(1)}, u32[]{:S(2)}, u32[]{:S(2)}) collective-permute-start(f32[2,8,64,256]{3,2,1,0:T(8,128)S(1)} %get-tuple-element.445), channel_id=1, source_target_pairs={{0,32},{32,64},{64,96},{96,128},{128,160},{160,192},{192,224},{1,3... | collective-permute-start | bytes 3145736 | tf_op jit(solution)/shard_map/while/body/eval_jaxpr/ppermute | solution.py:16
  347.6 1.0 copy-start.1
  348.6 25.7 %collective-permute-start = (f32[2,8,64,256]{3,2,1,0:T(8,128)S(1)}, f32[2,8,64,256]{3,2,1,0:T(8,128)S(1)}, u32[]{:S(2)}, u32[]{:S(2)}) collective-permute-start(f32[2,8,64,256]{3,2,1,0:T(8,128)S(1)} %get-tuple-element.445), channel_id=1, source_target_pairs={{0,32},{32,64},{64,96},{96,128},{128,160},{160,192},{192,224},{1,3... | collective-permute-start | bytes 3145736 | tf_op jit(solution)/shard_map/while/body/eval_jaxpr/ppermute | solution.py:16
  374.2 1.0 copy-start.1
  375.2 24.7 %collective-permute-start = (f32[2,8,64,256]{3,2,1,0:T(8,128)S(1)}, f32[2,8,64,256]{3,2,1,0:T(8,128)S(1)}, u32[]{:S(2)}, u32[]{:S(2)}) collective-permute-start(f32[2,8,64,256]{3,2,1,0:T(8,128)S(1)} %get-tuple-element.445), channel_id=1, source_target_pairs={{0,32},{32,64},{64,96},{96,128},{128,160},{160,192},{192,224},{1,3... | collective-permute-start | bytes 3145736 | tf_op jit(solution)/shard_map/while/body/eval_jaxpr/ppermute | solution.py:16
  399.9 1.0 copy-start.1
  400.9 23.8 %collective-permute-start = (f32[2,8,64,256]{3,2,1,0:T(8,128)S(1)}, f32[2,8,64,256]{3,2,1,0:T(8,128)S(1)}, u32[]{:S(2)}, u32[]{:S(2)}) collective-permute-start(f32[2,8,64,256]{3,2,1,0:T(8,128)S(1)} %get-tuple-element.445), channel_id=1, source_target_pairs={{0,32},{32,64},{64,96},{96,128},{128,160},{160,192},{192,224},{1,3... | collective-permute-start | bytes 3145736 | tf_op jit(solution)/shard_map/while/body/eval_jaxpr/ppermute | solution.py:16
  424.7 1.0 copy-start.1
  425.7 22.9 %collective-permute-start = (f32[2,8,64,256]{3,2,1,0:T(8,128)S(1)}, f32[2,8,64,256]{3,2,1,0:T(8,128)S(1)}, u32[]{:S(2)}, u32[]{:S(2)}) collective-permute-start(f32[2,8,64,256]{3,2,1,0:T(8,128)S(1)} %get-tuple-element.445), channel_id=1, source_target_pairs={{0,32},{32,64},{64,96},{96,128},{128,160},{160,192},{192,224},{1,3... | collective-permute-start | bytes 3145736 | tf_op jit(solution)/shard_map/while/body/eval_jaxpr/ppermute | solution.py:16
  448.6 1.0 copy-start.1
  449.6 22.0 %collective-permute-start = (f32[2,8,64,256]{3,2,1,0:T(8,128)S(1)}, f32[2,8,64,256]{3,2,1,0:T(8,128)S(1)}, u32[]{:S(2)}, u32[]{:S(2)}) collective-permute-start(f32[2,8,64,256]{3,2,1,0:T(8,128)S(1)} %get-tuple-element.445), channel_id=1, source_target_pairs={{0,32},{32,64},{64,96},{96,128},{128,160},{160,192},{192,224},{1,3... | collective-permute-start | bytes 3145736 | tf_op jit(solution)/shard_map/while/body/eval_jaxpr/ppermute | solution.py:16
  471.6 1.0 copy-start.1
  472.6 21.1 %collective-permute-start = (f32[2,8,64,256]{3,2,1,0:T(8,128)S(1)}, f32[2,8,64,256]{3,2,1,0:T(8,128)S(1)}, u32[]{:S(2)}, u32[]{:S(2)}) collective-permute-start(f32[2,8,64,256]{3,2,1,0:T(8,128)S(1)} %get-tuple-element.445), channel_id=1, source_target_pairs={{0,32},{32,64},{64,96},{96,128},{128,160},{160,192},{192,224},{1,3... | collective-permute-start | bytes 3145736 | tf_op jit(solution)/shard_map/while/body/eval_jaxpr/ppermute | solution.py:16
  493.6 1.0 copy-start.1
